TPU v7x, 256 devices: a whole 4x4x8 slice. The times are simulated.
256 devices in a mesh: tok: 16 (over z, x_lo), head: 16 (over x_hi, y, core).
Axes of the slice: x: 4 (x_hi: 2, x_lo: 2; x = x_hi * 2 + x_lo), y: 4, z: 8, core: 2. Of those that a mesh axis runs over, the one named last changes fastest.
Arguments:
- tri_tokens: bfloat16 [8192, 1024], P(('tok', 'head')), may hold values from -6 to 6
- image_tokens: bfloat16 [65536, 1024], P('tok'), may hold values from -6 to 6
- cross_q: bfloat16 [1024, 1024], P(None, 'head'), may hold values from -0.1875 to 0.1875
- cross_kv: bfloat16 [2, 1024, 1024], P(None, None, 'head'), may hold values from -0.1875 to 0.1875
- cross_out: bfloat16 [1024, 1024], P('head'), may hold values from -0.1875 to 0.1875
- self_qkv: bfloat16 [3, 1024, 1024], P(None, None, 'head'), may hold values from -0.1875 to 0.1875
- self_out: bfloat16 [1024, 1024], P('head'), may hold values from -0.1875 to 0.1875
- mlp_in: bfloat16 [1024, 4096], P(None, 'head'), may hold values from -0.1875 to 0.1875
- mlp_out: bfloat16 [4096, 1024], P('head'), may hold values from -0.09375 to 0.09375
Outputs:
- tri_out: bfloat16 [8192, 1024], P(('tok', 'head'))
All inputs are finite; a program needn't handle non-finite values.
Results may differ from a plain program's by a relative error of at most 0.013.
Values may be sent and summed in bfloat16 or wider, within the bound.
No kernel may reach another device: no remote copies, remote signals or barrier semaphores. Data moves between devices by JAX's collectives and lax.ppermute only.
A program may use at most 128 MiB of HBM per device.

v0:
```python
import math

import jax
import jax.numpy as jnp
from jax import lax
from jax.sharding import PartitionSpec as P

HEADS = 16


score_gain = 2.5


def layer_norm(values):
    centered = values - jnp.mean(values, axis=-1, keepdims=True)
    return centered * lax.rsqrt(jnp.mean(centered * centered, axis=-1, keepdims=True) + 1e-05)


def head_norm(values, head_count):
    shaped = values.reshape(values.shape[0], head_count, -1)
    normed = shaped * lax.rsqrt(jnp.mean(shaped * shaped, axis=-1, keepdims=True) + 1e-06)
    return normed.reshape(values.shape[0], -1).astype(jnp.bfloat16)


def partial_attention(queries, kv_rows, head_count):
    query_count = queries.shape[0]
    head_size = queries.shape[1] // head_count
    score_scale = score_gain / math.sqrt(head_size)
    query_block = math.gcd(query_count, 512)
    key_block = math.gcd(kv_rows.shape[0], 2048)
    query_blocks = queries.reshape(query_count // query_block, query_block, head_count, head_size)
    key_blocks = kv_rows.reshape(kv_rows.shape[0] // key_block, key_block, 2, head_count, head_size)

    def one_block(query_tile):

        def key_step(running, key_tile):
            weighted, totals = running
            scores = (
                jnp.einsum(
                    "qhd,khd->qhk", query_tile, key_tile[:, 0], preferred_element_type=jnp.float32
                )
                * score_scale
            )
            exp_scores = jnp.exp(scores)
            totals = totals + jnp.sum(exp_scores, axis=-1)
            weighted = weighted + jnp.einsum(
                "qhk,khd->qhd",
                exp_scores.astype(jnp.bfloat16),
                key_tile[:, 1],
                preferred_element_type=jnp.float32,
            )
            return ((weighted, totals), None)

        starting = (
            jnp.zeros((query_block, head_count, head_size), jnp.float32),
            jnp.zeros((query_block, head_count), jnp.float32),
        )
        result, _ = lax.scan(key_step, starting, key_blocks)
        return result

    weighted, totals = lax.map(one_block, query_blocks)
    return (
        weighted.reshape(query_count, head_count, head_size),
        totals.reshape(query_count, head_count),
    )


def finish(weighted, totals):
    return (weighted / totals[:, :, None]).reshape(weighted.shape[0], -1).astype(jnp.bfloat16)


def make_fold(queries, head_count, kv_piece):
    weighted, totals = partial_attention(queries, kv_piece, head_count)
    return (weighted, totals)


def per_device(
    tri_tokens, image_tokens, cross_q, cross_kv, cross_out, self_qkv, self_out, mlp_in, mlp_out
):
    head_width = cross_q.shape[1]
    head_size = tri_tokens.shape[1] // HEADS
    head_count = head_width // head_size

    def spread(normed, project):
        return project(lax.all_gather(normed, "head", axis=0, tiled=True), jnp.int32(0))

    def collect(operand, weight):
        return lax.psum_scatter(
            jnp.dot(operand, weight, preferred_element_type=jnp.float32).astype(jnp.bfloat16),
            "head",
            scatter_dimension=0,
            tiled=True,
        ).astype(jnp.float32)

    def project_cross(shard_rows, first_row):
        return head_norm(
            jnp.dot(shard_rows, cross_q, preferred_element_type=jnp.float32), head_count
        )

    stream_zero = tri_tokens.astype(jnp.float32)
    queries = spread(layer_norm(stream_zero).astype(jnp.bfloat16), project_cross)
    kv_weight = jnp.concatenate([cross_kv[0], cross_kv[1]], axis=1)
    image_kv = jnp.dot(image_tokens, kv_weight, preferred_element_type=jnp.float32)
    view_kv = jnp.concatenate(
        [
            head_norm(image_kv[:, :head_width], head_count),
            image_kv[:, head_width:].astype(jnp.bfloat16),
        ],
        axis=1,
    )
    weighted, totals = make_fold(
        queries, head_count, lax.all_gather(view_kv, "tok", axis=0, tiled=True)
    )
    stream_one = stream_zero + collect(finish(weighted, totals), cross_out)
    self_weight = jnp.concatenate([self_qkv[0], self_qkv[1], self_qkv[2]], axis=1)

    def project_self(shard_rows, first_row):
        mixed = jnp.dot(shard_rows, self_weight, preferred_element_type=jnp.float32)
        return jnp.concatenate(
            [
                head_norm(mixed[:, :head_width], head_count),
                head_norm(mixed[:, head_width : 2 * head_width], head_count),
                mixed[:, 2 * head_width :].astype(jnp.bfloat16),
            ],
            axis=1,
        )

    projected = spread(layer_norm(stream_one).astype(jnp.bfloat16), project_self)
    self_queries = projected[:, :head_width]
    self_kv = projected[:, head_width:]
    weighted, totals = make_fold(
        self_queries, head_count, lax.all_gather(self_kv, "tok", axis=0, tiled=True)
    )
    stream_two = stream_one + collect(finish(weighted, totals), self_out)

    def project_mlp(shard_rows, first_row):
        return jax.nn.gelu(
            jnp.dot(shard_rows, mlp_in, preferred_element_type=jnp.float32), approximate=True
        ).astype(jnp.bfloat16)

    hidden = spread(layer_norm(stream_two).astype(jnp.bfloat16), project_mlp)
    return (stream_two + collect(hidden, mlp_out)).astype(jnp.bfloat16)


def solution(mesh):
    return jax.shard_map(
        per_device,
        mesh=mesh,
        in_specs=(
            P(("tok", "head"), None),
            P("tok", None),
            P(None, "head"),
            P(None, None, "head"),
            P("head", None),
            P(None, None, "head"),
            P("head", None),
            P(None, "head"),
            P("head", None),
        ),
        out_specs=P(("tok", "head"), None),
        check_vma=False,
    )
```

profile of v0, /device:TPU:32, one launch (start us, length us, event | category | flops | bytes accessed | tf_op | source)
XLA Modules:
  0.0 1121.5 jit_solution(5238628317527319799)
XLA Ops:
  11.2 6.3 convolution_bitcast_fusion
  19.0 43.8 %all-gather.8.cloned.1.call-done = bf16[512,1024]{1,0:T(8,128)(2,1)} async-done(((bf16[32,1024]{1,0:T(8,128)(2,1)}), bf16[512,1024]{1,0:T(8,128)(2,1)}) %all-gather.8.cloned.1.call-update) | async-done | bytes 1048592 | tf_op jit(solution)/shard_map/all_gather | solution.py:85
  64.5 352.4 %all-gather.6.cloned.1.call-done = bf16[65536,128]{0,1:T(8,128)(2,1)} async-done(((bf16[4096,128]{0,1:T(8,128)(2,1)}), bf16[65536,128]{0,1:T(8,128)(2,1)}) %all-gather.6.cloned.1.call-update) | async-done | bytes 16777232 | tf_op jit(solution)/shard_map/all_gather | solution.py:112
  416.9 15.1 %copy.16 = bf16[16,8,32,2048]{3,2,1,0:T(8,128)(2,1)S(1)} copy(bf16[16,8,32,2048]{3,1,2,0:T(8,128)(2,1)} %bitcast.135) | data formatting | bytes 33554432
  432.0 21.0 %copy.14 = bf16[32,2048,2,1,64]{1,4,3,2,0:T(8,128)(2,1)} copy(bf16[32,2048,2,1,64]{1,0,4,2,3:T(8,128)(2,1)S(1)} %bitcast.134) | data formatting | bytes 33554432
  453.0 217.0 %while.50 = (s32[]{:T(128)}, f32[512,1,64]{0,2,1:T(8,128)S(1)}, f32[512,1]{0,1:T(1,128)S(1)}, bf16[32,2048,2,1,64]{1,4,3,2,0:T(8,128)(2,1)}, bf16[512,1,64]{0,2,1:T(8,128)(2,1)S(1)}, /*index=5*/s32[]{:T(128)}, s32[]{:T(128)}) while((s32[]{:T(128)}, f32[512,1,64]{0,2,1:T(8,128)S(1)}, f32[512,1]{0,1:T(1,128)S(1)}, ...), condition=%wide.region_6.0_spmd.clone, body=%wide.region_4.6_spmd.clone.sunk | while | flops 272695808 | bytes 10297436 | solution.py:58
  456.8 3.0 fusion.91
  463.6 3.0 fusion.91
  470.4 3.0 fusion.91
  477.1 3.0 fusion.91
  483.9 3.0 fusion.91
  490.7 3.0 fusion.91
  497.5 3.0 fusion.91
  504.3 3.0 fusion.91
  511.0 3.0 fusion.91
  524.6 3.0 fusion.91
  531.4 3.0 fusion.91
  538.2 3.0 fusion.91
  544.9 3.0 fusion.91
  671.5 78.9 %reduce-scatter.4.cloned.1.call-done = bf16[32,1024]{1,0:T(8,128)(2,1)} async-done(((bf16[512,1024]{1,0:T(8,128)(2,1)}), bf16[32,1024]{1,0:T(8,128)(2,1)}) %reduce-scatter.4.cloned.1.call-update) | async-done | bytes 65552 | tf_op jit(solution)/shard_map/reduce_scatter | solution.py:88
  754.1 49.0 %all-gather.10.cloned.1.call-done = bf16[512,1024]{1,0:T(8,128)(2,1)} async-done(((bf16[32,1024]{1,0:T(8,128)(2,1)}), bf16[512,1024]{1,0:T(8,128)(2,1)}) %all-gather.10.cloned.1.call-update) | async-done | bytes 1048592 | tf_op jit(solution)/shard_map/all_gather | solution.py:85
  805.9 70.5 %all-gather.12.cloned.1.call-done = bf16[8192,128]{0,1:T(8,128)(2,1)} async-done(((bf16[512,128]{0,1:T(8,128)(2,1)}), bf16[8192,128]{0,1:T(8,128)(2,1)}) %all-gather.12.cloned.1.call-update) | async-done | bytes 2097168 | tf_op jit(solution)/shard_map/all_gather | solution.py:132
  876.4 4.5 reshape.193
  883.7 23.0 %while.51 = (s32[]{:T(128)}, f32[512,1,64]{0,2,1:T(8,128)S(1)}, f32[512,1]{0,1:T(1,128)S(1)}, bf16[4,2048,2,1,64]{1,4,3,2,0:T(8,128)(2,1)S(1)}, bf16[512,1,64]{0,2,1:T(8,128)(2,1)S(1)}, /*index=5*/s32[]{:T(128)}, s32[]{:T(128)}) while((s32[]{:T(128)}, f32[512,1,64]{0,2,1:T(8,128)S(1)}, f32[512,1]{0,1:T(1,128)S(1)}, ...), condition=%wide.region_14.15_spmd.clone, body=%wide.region_12.14_spmd.clone.sunk | while | flops 272695808 | bytes 10297436 | solution.py:58
  886.4 3.0 fusion.95
  892.2 3.0 fusion.95
  897.9 3.0 fusion.95
  903.7 3.0 fusion.95
  909.1 73.8 %reduce-scatter.6.cloned.1.call-done = bf16[32,1024]{1,0:T(8,128)(2,1)} async-done(((bf16[512,1024]{1,0:T(8,128)(2,1)}), bf16[32,1024]{1,0:T(8,128)(2,1)}) %reduce-scatter.6.cloned.1.call-update) | async-done | bytes 65552 | tf_op jit(solution)/shard_map/reduce_scatter | solution.py:88
  986.7 49.1 %all-gather.14.cloned.1.call-done = bf16[512,1024]{1,0:T(8,128)(2,1)} async-done(((bf16[32,1024]{1,0:T(8,128)(2,1)}), bf16[512,1024]{1,0:T(8,128)(2,1)}) %all-gather.14.cloned.1.call-update) | async-done | bytes 1048592 | tf_op jit(solution)/shard_map/all_gather | solution.py:85
  1035.8 3.6 convolution_convert_fusion
  1039.4 73.7 %reduce-scatter.8.cloned.1.call-done = bf16[32,1024]{1,0:T(8,128)(2,1)} async-done(((bf16[512,1024]{1,0:T(8,128)(2,1)}), bf16[32,1024]{1,0:T(8,128)(2,1)}) %reduce-scatter.8.cloned.1.call-update) | async-done | bytes 65552 | tf_op jit(solution)/shard_map/reduce_scatter | solution.py:88
  (196 shorter events, 214.6 us)
Async XLA Ops:
  6.5 1029.2 %copy-start = (bf16[256,1024]{1,0:T(8,128)(2,1)S(1)}, bf16[256,1024]{1,0:T(8,128)(2,1)}, u32[]{:S(2)}) copy-start(bf16[256,1024]{1,0:T(8,128)(2,1)} %param.21) | copy-start | bytes 1572868
  6.5 56.3 %all-gather.8.cloned.1.call-start = ((), (), s32[]{:S(2)}) async-start(), calls=%async_computation.4 | async-start | bytes 1114112 | tf_op jit(solution)/shard_map/all_gather | solution.py:85
  10.2 406.7 %all-gather.6.cloned.1.call-start = ((), (), s32[]{:S(2)}) async-start(), calls=%async_computation.3 | async-start | bytes 17825792 | tf_op jit(solution)/shard_map/all_gather | solution.py:112
  17.5 45.3 %copy-start.5 = (bf16[1024,64]{0,1:T(8,128)(2,1)S(1)}, bf16[1024,64]{0,1:T(8,128)(2,1)}, u32[]{:S(2)}) copy-start(bf16[1024,64]{0,1:T(8,128)(2,1)} %param.15) | copy-start | bytes 393220
  18.9 731.5 %reduce-scatter.4.cloned.1.call-start = ((), (), s32[]{:S(2)}) async-start(), calls=%async_computation.5 | async-start | bytes 1114112 | tf_op jit(solution)/shard_map/reduce_scatter | solution.py:88
  453.0 217.0 %copy-start.6 = (bf16[64,1024]{1,0:T(8,128)(2,1)S(1)}, bf16[64,1024]{1,0:T(8,128)(2,1)}, u32[]{:S(2)}) copy-start(bf16[64,1024]{1,0:T(8,128)(2,1)} %param.17) | copy-start | bytes 393220
  453.0 297.4 %copy-start.1 = (bf16[32,1024]{1,0:T(8,128)(2,1)S(1)}, bf16[32,1024]{1,0:T(8,128)(2,1)}, u32[]{:S(2)}) copy-start(bf16[32,1024]{1,0:T(8,128)(2,1)} %param.13) | copy-start | bytes 196612
  453.0 301.1 %copy-start.4 = (bf16[3,1024,64]{1,2,0:T(8,128)(2,1)S(1)}, bf16[3,1024,64]{1,2,0:T(8,128)(2,1)}, u32[]{:S(2)}) copy-start(bf16[3,1024,64]{1,2,0:T(8,128)(2,1)} %param.18) | copy-start | bytes 1179652
  671.4 131.7 %all-gather.10.cloned.1.call-start = ((), (), s32[]{:S(2)}) async-start(), calls=%async_computation.6 | async-start | bytes 1114112 | tf_op jit(solution)/shard_map/all_gather | solution.py:85
  754.0 122.4 %all-gather.12.cloned.1.call-start = ((), (), s32[]{:S(2)}) async-start(), calls=%async_computation.7 | async-start | bytes 2228224 | tf_op jit(solution)/shard_map/all_gather | solution.py:132
  805.6 177.3 %reduce-scatter.6.cloned.1.call-start = ((), (), s32[]{:S(2)}) async-start(), calls=%async_computation.8 | async-start | bytes 1114112 | tf_op jit(solution)/shard_map/reduce_scatter | solution.py:88
  883.7 99.3 %copy-start.2 = (bf16[32,1024]{1,0:T(8,128)(2,1)S(1)}, bf16[32,1024]{1,0:T(8,128)(2,1)}, u32[]{:S(2)}) copy-start(bf16[32,1024]{1,0:T(8,128)(2,1)} %reduce-scatter.4.cloned.1.call-done) | copy-start | bytes 196612
  909.1 126.7 %all-gather.14.cloned.1.call-start = ((), (), s32[]{:S(2)}) async-start(), calls=%async_computation.9 | async-start | bytes 1114112 | tf_op jit(solution)/shard_map/all_gather | solution.py:85
  983.0 130.2 %copy-start.3 = (bf16[32,1024]{1,0:T(8,128)(2,1)S(1)}, bf16[32,1024]{1,0:T(8,128)(2,1)}, u32[]{:S(2)}) copy-start(bf16[32,1024]{1,0:T(8,128)(2,1)} %reduce-scatter.6.cloned.1.call-done) | copy-start | bytes 196612
  986.6 126.5 %reduce-scatter.8.cloned.1.call-start = ((), (), s32[]{:S(2)}) async-start(), calls=%async_computation.10 | async-start | bytes 1114112 | tf_op jit(solution)/shard_map/reduce_scatter | solution.py:88
Sparse Core Ops, SparseCore 0:
  10.3 52.4 all-gather.7
  64.6 352.2 all-gather.5
  671.6 78.7 reduce-scatter.3
  754.1 48.9 all-gather.9
  805.8 70.6 all-gather.11
  909.2 73.7 reduce-scatter.5
  986.8 48.9 all-gather.13
  1039.8 73.2 reduce-scatter.7
where the time goes:
time: 1130 us; the launch traced here: 1120 us
  waiting for transfers between devices  791 us (70%)
  matrix products  221 us (20%)
  local copies, waits for them, and re-layouts  79.2 us (7%)
  other arithmetic  14.9 us (1%)
  between operations  13.7 us (1%)
    all_gather x1, waiting for transfers between devices, per_device(): lax.all_gather(view_kv, 'tok', axis=0, tiled=True)  352 us
    reduce_scatter x3, waiting for transfers between devices, collect(): lax.psum_scatter(jnp.dot(operand, weight, preferred_element_type=jnp.floa...  226 us
    all_gather x3, waiting for transfers between devices, spread(): lax.all_gather(normed, 'head', axis=0, tiled=True)  142 us
    dot_general x36, matrix products, key_step(): jnp.einsum('qhk,khd->qhd', exp_scores.astype(jnp.bfloat16), key_tile[:, 1...  107 us
    dot_general x36, matrix products, key_step(): jnp.einsum('qhd,khd->qhk', query_tile, key_tile[:, 0], preferred_element_...  96.9 us
    all_gather x1, waiting for transfers between devices, per_device(): lax.all_gather(self_kv, 'tok', axis=0, tiled=True)  70.5 us
    unnamed x17, local copies, waits for them, and re-layouts  38.8 us
    squeeze x36, local copies, waits for them, and re-layouts, one_block(): result, _ = lax.scan(key_step, starting, key_blocks)  34.8 us
  transfers between devices with their start and end apart: 8, of which 8 were waited for; matrix products, arithmetic and copies ran while one was open for 1% of the time, Pallas kernels for 0%

commit v1 on v0

v1 whole, which is shorter than its diff:
```python
import functools
import math

import jax
import jax.numpy as jnp
from jax import lax
from jax.experimental import pallas as pl
from jax.experimental.pallas import tpu as pltpu
from jax.sharding import Mesh, PartitionSpec as P

HEAD_SIZE = 64
EXT = 80
SCORE = 2.5 / math.sqrt(HEAD_SIZE) * math.log2(math.e)
PLANE = ("xh", "y")
HEAD = ("xh", "y", "c")


def layer_norm(values):
    centered = values - jnp.mean(values, axis=-1, keepdims=True)
    return centered * lax.rsqrt(jnp.mean(centered * centered, axis=-1, keepdims=True) + 1e-05)


def column_norm(values):
    return values * lax.rsqrt(jnp.mean(values * values, axis=0, keepdims=True) + 1e-06)


def project_kv_kernel(image_ref, weight_ref, out_ref):
    product = jnp.dot(image_ref[...], weight_ref[...], preferred_element_type=jnp.float32).T
    out_ref[:HEAD_SIZE] = column_norm(product[:HEAD_SIZE]).astype(jnp.bfloat16)
    out_ref[HEAD_SIZE:] = product[HEAD_SIZE:].astype(jnp.bfloat16)


def project_kv(image_tokens, weight):
    rows, features = image_tokens.shape
    block = 512
    return pl.pallas_call(
        project_kv_kernel,
        grid=(rows // block,),
        in_specs=[
            pl.BlockSpec((block, features), lambda i: (i, 0)),
            pl.BlockSpec(weight.shape, lambda i: (0, 0)),
        ],
        out_specs=pl.BlockSpec((2 * HEAD_SIZE, block), lambda i: (0, i)),
        out_shape=jax.ShapeDtypeStruct((2 * HEAD_SIZE, rows), jnp.bfloat16),
        compiler_params=pltpu.CompilerParams(vmem_limit_bytes=32 * 2**20),
        name="project_kv",
    )(image_tokens, weight)


def attention_kernel(step, piece_count, query_ref, *refs):
    pieces = refs[:piece_count]
    out_ref, keys, values = refs[piece_count:]
    width = pieces[0].shape[-1]

    @pl.when(pl.program_id(0) == 0)
    def _():
        first = 0
        for piece in pieces:
            for i in range(piece.shape[0]):
                keys[first : first + width, :] = piece[i, :HEAD_SIZE].T
                values[:HEAD_SIZE, first : first + width] = piece[i, HEAD_SIZE:]
                first += width
        row = lax.broadcasted_iota(jnp.int32, (EXT - HEAD_SIZE, values.shape[1]), 0)
        values[HEAD_SIZE:] = jnp.where(row == 0, 1.0, 0.0).astype(jnp.bfloat16)

    queries = query_ref[...]
    total = jnp.zeros((EXT, queries.shape[1]), jnp.float32)
    for first in range(0, keys.shape[0], step):
        scores = jnp.dot(
            keys[first : first + step, :], queries, preferred_element_type=jnp.float32
        )
        weights = jnp.exp2(scores).astype(jnp.bfloat16)
        total = total + jnp.dot(
            values[:, first : first + step], weights, preferred_element_type=jnp.float32
        )
    out_ref[...] = total.astype(out_ref.dtype)


def attention(queries, pieces, step=1024):
    blocks, _, width = queries.shape
    key_count = sum(piece.shape[0] * piece.shape[2] for piece in pieces)
    return pl.pallas_call(
        functools.partial(attention_kernel, step, len(pieces)),
        grid=(blocks,),
        in_specs=[pl.BlockSpec((None, HEAD_SIZE, width), lambda i: (i, 0, 0))]
        + [pl.BlockSpec(piece.shape, lambda i: (0, 0, 0)) for piece in pieces],
        out_specs=pl.BlockSpec((None, EXT, width), lambda i: (i, 0, 0)),
        out_shape=jax.ShapeDtypeStruct((blocks, EXT, width), jnp.bfloat16),
        scratch_shapes=[
            pltpu.VMEM((key_count, HEAD_SIZE), jnp.bfloat16),
            pltpu.VMEM((EXT, key_count), jnp.bfloat16),
        ],
        compiler_params=pltpu.CompilerParams(vmem_limit_bytes=48 * 2**20),
        name="attention",
    )(queries, *pieces)


def exchange(values, axes):
    return lax.all_to_all(values, axes, 0, 0, tiled=True)


def share(values, axes, count):
    return exchange(jnp.broadcast_to(values, (count,) + values.shape), axes)


def share_head(values, plane):
    return lax.all_gather(share(values, PLANE, plane), "c", axis=1)


def finish(partials):
    total = jnp.sum(partials.astype(jnp.float32), axis=0)
    return (total[:HEAD_SIZE] / total[HEAD_SIZE : HEAD_SIZE + 1]).astype(jnp.bfloat16)


def across(left, right, dims):
    return lax.dot_general(left, right, (dims, ((), ())), preferred_element_type=jnp.float32)


def per_device(
    sizes,
    tri_tokens,
    image_tokens,
    cross_q,
    cross_kv,
    cross_out,
    self_qkv,
    self_out,
    mlp_in,
    mlp_out,
):
    width = tri_tokens.shape[1]
    plane = sizes["xh"] * sizes["y"]
    rows = tri_tokens.shape[0] * plane * sizes["c"]

    cross_out_all = lax.all_gather(cross_out, HEAD, axis=0, tiled=True)
    self_out_all = lax.all_gather(self_out, HEAD, axis=0, tiled=True)

    tri_group = share_head(tri_tokens, plane).reshape(rows, width)
    image_kv = project_kv(image_tokens, jnp.concatenate([cross_kv[0], cross_kv[1]], axis=1))
    other_kv = lax.ppermute(image_kv, "xl", [(0, 1), (1, 0)])
    stream_zero = tri_group.astype(jnp.float32)
    normed = layer_norm(stream_zero).astype(jnp.bfloat16)
    queries = (column_norm(across(cross_q, normed, ((0,), (1,)))) * SCORE).astype(jnp.bfloat16)
    z_axes = ("za", "zb")
    z_count = sizes["za"] * sizes["zb"]
    all_queries = share(queries, z_axes, z_count)
    partials = attention(all_queries, [image_kv[None], other_kv[None]])
    mix = finish(exchange(partials, z_axes))
    mix_all = share_head(mix, plane).reshape(width, rows)
    stream_one = stream_zero + across(mix_all, cross_out_all, ((0,), (0,)))

    normed = layer_norm(stream_one).astype(jnp.bfloat16)
    self_weight = jnp.concatenate([self_qkv[0], self_qkv[1], self_qkv[2]], axis=1)
    mixed = across(self_weight, normed, ((0,), (1,)))
    queries = (column_norm(mixed[:HEAD_SIZE]) * SCORE).astype(jnp.bfloat16)
    self_kv = jnp.concatenate(
        [
            column_norm(mixed[HEAD_SIZE : 2 * HEAD_SIZE]).astype(jnp.bfloat16),
            mixed[2 * HEAD_SIZE :].astype(jnp.bfloat16),
        ],
        axis=0,
    )
    pair = ("zb", "xl")
    all_kv = share(self_kv, "za", sizes["za"])
    all_queries = share(queries, pair, sizes["zb"] * sizes["xl"])
    partials = attention(all_queries, [all_kv])
    mix = finish(exchange(partials, pair))
    mix_all = share_head(mix, plane).reshape(width, rows)
    stream_two = stream_one + across(mix_all, self_out_all, ((0,), (0,)))

    normed = layer_norm(stream_two).astype(jnp.bfloat16)
    hidden = jax.nn.gelu(
        jnp.dot(normed, mlp_in, preferred_element_type=jnp.float32), approximate=True
    ).astype(jnp.bfloat16)
    product = jnp.dot(hidden, mlp_out, preferred_element_type=jnp.float32)
    product = product.astype(jnp.bfloat16).reshape(plane, sizes["c"], -1, width)
    core = lax.axis_index("c")
    kept = lax.dynamic_index_in_dim(product, core, 1, keepdims=False)
    given = lax.dynamic_index_in_dim(product, 1 - core, 1, keepdims=False)
    got = lax.ppermute(given, "c", [(0, 1), (1, 0)])
    both = (kept.astype(jnp.float32) + got.astype(jnp.float32)).astype(jnp.bfloat16)
    collected = jnp.sum(exchange(both, PLANE).astype(jnp.float32), axis=0)
    place = lax.axis_index(HEAD) * tri_tokens.shape[0]
    own = lax.dynamic_slice_in_dim(stream_two, place, tri_tokens.shape[0], axis=0)
    return (own + collected).astype(jnp.bfloat16)


def solution(mesh):
    sizes = {"za": 4, "zb": 2, "xl": 2, "xh": 2, "y": 4, "c": 2}
    names = tuple(sizes)
    fine = Mesh(mesh.devices.reshape(tuple(sizes.values())), names)
    tok = ("za", "zb", "xl")
    return jax.shard_map(
        functools.partial(per_device, sizes),
        mesh=fine,
        in_specs=(
            P(names, None),
            P(tok, None),
            P(None, HEAD),
            P(None, None, HEAD),
            P(HEAD, None),
            P(None, None, HEAD),
            P(HEAD, None),
            P(None, HEAD),
            P(HEAD, None),
        ),
        out_specs=P(names, None),
        check_vma=False,
    )
```

time: 1130 us -> 265 us (0.23)
  waiting for transfers between devices: 791 us -> 57.7 us
  matrix products: 221 us -> 10.8 us
  blocking collectives: 0 us -> 107 us
  local copies, waits for them, and re-layouts: 79.2 us -> 8.05 us
  Pallas kernels: 0 us -> 39 us
  starting transfers between devices: 0.48 us -> 19.5 us
    all_gather x5, waiting for transfers between devices: 565 us -> 22.5 us  [the longest x3 22.4 us: share_head(): return lax.all_gather(share(values, PLANE, plane), 'c', axis=1)]
    reduce_scatter x3 -> x0, waiting for transfers between devices: 226 us -> none  [collect(): lax.psum_scatter(jnp.dot(operand, weight, preferred_element_type=jnp.floa...]
    dot_general x78 -> x5, matrix products: 221 us -> 10.8 us  [the longest x4 7.91 us: across(): lax.dot_general(left, right, (dims, ((), ())), preferred_element_type=jnp...]
    all_to_all x0 -> x6, blocking collectives: none -> 107 us  [exchange(): return lax.all_to_all(values, axes, 0, 0, tiled=True)]
    pallas_call x0 -> x3, Pallas kernels: none -> 39 us  [the longest x2 34.8 us: attention(): pl.pallas_call(functools.partial(attention_kernel, step, len(pieces)), gr...]
    squeeze x37 -> x1, local copies, waits for them, and re-layouts: 35.8 us -> 0.04 us  [per_device(): given = lax.dynamic_index_in_dim(product, 1 - core, 1, keepdims=False)]
    unnamed x17 -> x16, local copies, waits for them, and re-layouts: 38.8 us -> 5.06 us
    all_to_all x0 -> x3, waiting for transfers between devices: none -> 28.5 us  [exchange(): return lax.all_to_all(values, axes, 0, 0, tiled=True)]
  transfers between devices with their start and end apart: 8 -> 10, of which waited for: 8 -> 8; matrix products, arithmetic and copies ran while one was open for 1% -> 5% of each run, Pallas kernels for 0% -> 15%
where the time goes in v1:
time: 265 us; the launch traced here: 264 us
  blocking collectives  107 us (40%)
  waiting for transfers between devices  57.7 us (22%)
  Pallas kernels  39 us (15%)
  starting transfers between devices  19.5 us (7%)
  between operations  13.5 us (5%)
  matrix products  10.8 us (4%)
  other arithmetic  8.38 us (3%)
  local copies, waits for them, and re-layouts  8.05 us (3%)
    all_to_all x6, blocking collectives, exchange(): return lax.all_to_all(values, axes, 0, 0, tiled=True)  107 us
    pallas_call x2, Pallas kernels, attention(): pl.pallas_call(functools.partial(attention_kernel, step, len(pieces)), gr...  34.8 us
    all_to_all x3, waiting for transfers between devices, exchange(): return lax.all_to_all(values, axes, 0, 0, tiled=True)  28.5 us
    all_gather x3, waiting for transfers between devices, share_head(): return lax.all_gather(share(values, PLANE, plane), 'c', axis=1)  22.4 us
    all_to_all x3, starting transfers between devices, exchange(): return lax.all_to_all(values, axes, 0, 0, tiled=True)  18.4 us
    dot_general x4, matrix products, across(): lax.dot_general(left, right, (dims, ((), ())), preferred_element_type=jnp...  7.91 us
  transfers between devices with their start and end apart: 10, of which 8 were waited for; matrix products, arithmetic and copies ran while one was open for 5% of the time, Pallas kernels for 15%

profile of v1, /device:TPU:32, one launch (start us, length us, event | category | flops | bytes accessed | tf_op | source)
XLA Modules:
  0.0 263.8 jit_solution(6935291496878424255)
XLA Ops:
  6.5 1.0 broadcast_in_dim.16
  7.5 18.4 %all_to_all.45 = bf16[8,32,1024]{2,1,0:T(8,128)(2,1)} all-to-all(bf16[8,32,1024]{2,1,0:T(8,128)(2,1)S(1)} %broadcast_in_dim.16), channel_id=1, replica_groups=mesh['za'=4,'zb'=2,'xl'=2,'xh'=2,'y'=4,'c'=2] {'xh','y'}, dimensions={0} | all-to-all | bytes 1048576 | tf_op jit(solution)/shard_map/all_to_all | solution.py:99
  26.5 3.4 %copy-done.1 = bf16[4096,1024]{1,0:T(8,128)(2,1)S(1)} copy-done((bf16[4096,1024]{1,0:T(8,128)(2,1)S(1)}, bf16[4096,1024]{1,0:T(8,128)(2,1)}, u32[]{:S(2)}) %copy-start.1) | copy-done | bytes 8388632
  29.9 4.2 %project_kv.1 = bf16[128,4096]{1,0:T(8,128)(2,1)S(1)} custom-call(bf16[4096,1024]{1,0:T(8,128)(2,1)S(1)} %copy-done.1, bf16[1024,128]{1,0:T(8,128)(2,1)S(1)} %pad_maximum_fusion.weight_ref), custom_call_target="tpu_custom_call" | custom-call | tf_op jit(solution)/shard_map/project_kv/pallas_call | solution.py:36
  34.8 4.1 %all-gather.13.cloned.1.call-done = bf16[8,64,1024]{2,1,0:T(8,128)(2,1)} async-done(((bf16[8,32,1024]{2,1,0:T(8,128)(2,1)}), bf16[8,64,1024]{2,1,0:T(8,128)(2,1)}) %all-gather.13.cloned.1.call-update) | async-done | bytes 1048592 | tf_op jit(solution)/shard_map/all_gather | solution.py:107
  38.9 1.4 convert_reduce_fusion
  40.4 1.6 multiply_reduce_fusion.2
  42.2 1.5 fusion.1
  44.3 0.8 broadcast_in_dim.34
  45.1 7.5 %all-to-all-start.1 = ((bf16[8,64,512]{2,1,0:T(8,128)(2,1)}), bf16[8,64,512]{2,1,0:T(8,128)(2,1)S(1)}, u32[]{:S(2)}, u32[]{:S(2)}) async-start(bf16[8,64,512]{2,1,0:T(8,128)(2,1)} %broadcast_in_dim.34), calls=%async_computation.1 | async-start | bytes 1048576 | tf_op jit(solution)/shard_map/all_to_all | solution.py:99
  52.6 4.6 %collective-permute-done = bf16[128,4096]{1,0:T(8,128)(2,1)S(1)} collective-permute-done((bf16[128,4096]{1,0:T(8,128)(2,1)S(1)}, bf16[128,4096]{1,0:T(8,128)(2,1)S(1)}, u32[]{:S(2)}, u32[]{:S(2)}) %collective-permute-start) | collective-permute-done | bytes 1048608 | tf_op jit(solution)/shard_map/ppermute | solution.py:140
  57.2 11.9 %all-to-all-done.1.query_ref = bf16[8,64,512]{2,1,0:T(8,128)(2,1)S(1)} async-done(((bf16[8,64,512]{2,1,0:T(8,128)(2,1)}), bf16[8,64,512]{2,1,0:T(8,128)(2,1)S(1)}, u32[]{:S(2)}, u32[]{:S(2)}) %all-to-all-start.1) | async-done | bytes 524320 | tf_op jit(solution)/shard_map/all_to_all | solution.py:99
  69.1 30.4 %attention.2 = bf16[8,80,512]{2,1,0:T(8,128)(2,1)S(1)} custom-call(bf16[8,64,512]{2,1,0:T(8,128)(2,1)S(1)} %all-to-all-done.1.query_ref, bf16[1,128,4096]{2,1,0:T(8,128)(2,1)S(1)} %bitcast.39, bf16[1,128,4096]{2,1,0:T(8,128)(2,1)S(1)} %bitcast.40), custom_call_target="tpu_custom_call" | custom-call | tf_op jit(solution)/shard_map/attention/pallas_call | solution.py:82
  99.6 23.3 %all_to_all.46 = bf16[8,80,512]{2,1,0:T(8,128)(2,1)S(1)} all-to-all(bf16[8,80,512]{2,1,0:T(8,128)(2,1)S(1)} %attention.2), channel_id=1, replica_groups=mesh['za'=4,'zb'=2,'xl'=2,'xh'=2,'y'=4,'c'=2] {'za','zb'}, dimensions={0} | all-to-all | bytes 1310720 | tf_op jit(solution)/shard_map/all_to_all | solution.py:99
  123.1 17.2 %all_to_all.47 = bf16[8,64,512]{2,1,0:T(8,128)(2,1)} all-to-all(bf16[8,64,512]{2,1,0:T(8,128)(2,1)S(1)} %broadcast_in_dim.37), channel_id=1, replica_groups=mesh['za'=4,'zb'=2,'xl'=2,'xh'=2,'y'=4,'c'=2] {'xh','y'}, dimensions={0} | all-to-all | bytes 1048576 | tf_op jit(solution)/shard_map/all_to_all | solution.py:99
  140.9 7.7 %all-gather.15.cloned.1.call-done = bf16[8,128,512]{2,1,0:T(8,128)(2,1)} async-done(((bf16[8,64,512]{2,1,0:T(8,128)(2,1)}), bf16[8,128,512]{2,1,0:T(8,128)(2,1)}) %all-gather.15.cloned.1.call-update) | async-done | bytes 1048592 | tf_op jit(solution)/shard_map/all_gather | solution.py:107
  148.6 3.5 %fusion.35 = (f32[512]{0:T(512)S(1)}, f32[512,1024]{1,0:T(8,128)S(1)}) fusion(bf16[1024,512]{1,0:T(8,128)(2,1)} %bitcast.46, bf16[1024,1024]{1,0:T(8,128)(2,1)} %all-gather.9.cloned.1.call-done, bf16[8,64,1024]{2,1,0:T(8,128)(2,1)} %all-gather.13.cloned.1.call-done), kind=kOutput, calls=%fused_computation.75 | convolution fusion | flops 1075314176 | bytes 6293504 | tf_op jit(solution)/shard_map/dot_general | solution.py:116
  154.0 4.2 %all-to-all-start.4 = ((bf16[4,64,512]{2,1,0:T(8,128)(2,1)}), bf16[4,64,512]{2,1,0:T(8,128)(2,1)S(1)}, u32[]{:S(2)}, u32[]{:S(2)}) async-start(bf16[4,64,512]{2,1,0:T(8,128)(2,1)} %broadcast_in_dim.38), calls=%async_computation.4 | async-start | bytes 524288 | tf_op jit(solution)/shard_map/all_to_all | solution.py:99
  158.2 5.2 %all-to-all-done.4.query_ref = bf16[4,64,512]{2,1,0:T(8,128)(2,1)S(1)} async-done(((bf16[4,64,512]{2,1,0:T(8,128)(2,1)}), bf16[4,64,512]{2,1,0:T(8,128)(2,1)S(1)}, u32[]{:S(2)}, u32[]{:S(2)}) %all-to-all-start.4) | async-done | bytes 262176 | tf_op jit(solution)/shard_map/all_to_all | solution.py:99
  163.5 22.9 %all_to_all.48.refs_0_ = bf16[4,128,512]{2,1,0:T(8,128)(2,1)S(1)} all-to-all(bf16[4,128,512]{2,1,0:T(8,128)(2,1)S(1)} %broadcast_in_dim.39), channel_id=1, replica_groups=mesh['za'=4,'zb'=2,'xl'=2,'xh'=2,'y'=4,'c'=2] {'za'}, dimensions={0} | all-to-all | bytes 1048576 | tf_op jit(solution)/shard_map/all_to_all | solution.py:99
  186.3 4.3 %attention.3 = bf16[4,80,512]{2,1,0:T(8,128)(2,1)S(1)} custom-call(bf16[4,64,512]{2,1,0:T(8,128)(2,1)S(1)} %all-to-all-done.4.query_ref, bf16[4,128,512]{2,1,0:T(8,128)(2,1)S(1)} %all_to_all.48.refs_0_), custom_call_target="tpu_custom_call" | custom-call | tf_op jit(solution)/shard_map/attention/pallas_call | solution.py:82
  190.7 8.4 %all_to_all.49 = bf16[4,80,512]{2,1,0:T(8,128)(2,1)S(1)} all-to-all(bf16[4,80,512]{2,1,0:T(8,128)(2,1)S(1)} %attention.3), channel_id=1, replica_groups=mesh['za'=4,'zb'=2,'xl'=2,'xh'=2,'y'=4,'c'=2] {'zb','xl'}, dimensions={0} | all-to-all | bytes 655360 | tf_op jit(solution)/shard_map/all_to_all | solution.py:99
  199.2 16.7 %all_to_all.50 = bf16[8,64,512]{2,1,0:T(8,128)(2,1)} all-to-all(bf16[8,64,512]{2,1,0:T(8,128)(2,1)S(1)} %broadcast_in_dim.40), channel_id=1, replica_groups=mesh['za'=4,'zb'=2,'xl'=2,'xh'=2,'y'=4,'c'=2] {'xh','y'}, dimensions={0} | all-to-all | bytes 1048576 | tf_op jit(solution)/shard_map/all_to_all | solution.py:99
  216.0 10.6 %all-gather.17.cloned.1.call-done = bf16[8,128,512]{2,1,0:T(8,128)(2,1)} async-done(((bf16[8,64,512]{2,1,0:T(8,128)(2,1)}), bf16[8,128,512]{2,1,0:T(8,128)(2,1)}) %all-gather.17.cloned.1.call-update) | async-done | bytes 1048592 | tf_op jit(solution)/shard_map/all_gather | solution.py:107
  226.6 3.3 %fusion.36 = (f32[512]{0:T(512)S(1)}, f32[512,1024]{1,0:T(8,128)S(1)}) fusion(f32[512,1024]{1,0:T(8,128)S(1)} %get-tuple-element.17, bf16[1024,512]{1,0:T(8,128)(2,1)} %bitcast.49, bf16[1024,1024]{1,0:T(8,128)(2,1)} %all-gather.11.cloned.1.call-done), kind=kOutput, calls=%fused_computation.76 | convolution fusion | flops 1074789888 | bytes 7342080 | tf_op jit(solution)/shard_map/dot_general | solution.py:116
  229.9 1.3 copy-done.2
  231.6 2.9 %convolution_convert_fusion = bf16[512,1024]{1,0:T(8,128)(2,1)S(1)} fusion(bf16[256,1024]{1,0:T(8,128)(2,1)S(1)} %copy-done, bf16[1024,256]{1,0:T(8,128)(2,1)S(1)} %copy-done.6, f32[512,1024]{1,0:T(8,128)} %copy-done.2, f32[512]{0:T(512)S(1)} %add_rsqrt_fusion.1, f32[512]{0:T(512)S(1)} %broadcast_multiply_fusion.1), kind=kOutput, calls=%fused_computation.11 | convolution fusion | flops 540147712 | bytes 4198400 | tf_op jit(solution)/shard_map/dot_general | solution.py:175
  234.9 1.6 collective-permute-done.1
  236.5 1.0 fusion.4
  237.5 6.7 %all-to-all-start.8 = ((bf16[8,32,1024]{2,1,0:T(8,128)(2,1)}), bf16[8,32,1024]{2,1,0:T(8,128)(2,1)S(1)}, u32[]{:S(2)}, u32[]{:S(2)}) async-start(bf16[8,32,1024]{2,1,0:T(8,128)(2,1)} %fusion.4), calls=%async_computation.8 | async-start | bytes 1048576 | tf_op jit(solution)/shard_map/all_to_all | solution.py:99
  244.2 11.4 %all-to-all-done.8 = bf16[8,32,1024]{2,1,0:T(8,128)(2,1)S(1)} async-done(((bf16[8,32,1024]{2,1,0:T(8,128)(2,1)}), bf16[8,32,1024]{2,1,0:T(8,128)(2,1)S(1)}, u32[]{:S(2)}, u32[]{:S(2)}) %all-to-all-start.8) | async-done | bytes 524320 | tf_op jit(solution)/shard_map/all_to_all | solution.py:99
  255.7 1.6 add_convert_fusion
  (63 shorter events, 5.7 us)
Async XLA Ops:
  6.5 225.0 %copy-start = (bf16[256,1024]{1,0:T(8,128)(2,1)S(1)}, bf16[256,1024]{1,0:T(8,128)(2,1)}, u32[]{:S(2)}) copy-start(bf16[256,1024]{1,0:T(8,128)(2,1)} %param.17) | copy-start | bytes 1572868
  6.5 19.4 %copy-start.4 = (bf16[2,1024,64]{1,2,0:T(8,128)(2,1)S(1)}, bf16[2,1024,64]{1,2,0:T(8,128)(2,1)}, u32[]{:S(2)}) copy-start(bf16[2,1024,64]{1,2,0:T(8,128)(2,1)} %param.12) | copy-start | bytes 786436
  6.5 32.3 %all-gather.13.cloned.1.call-start = ((), (), s32[]{:S(2)}) async-start(), calls=%async_computation.11 | async-start | bytes 1572864 | tf_op jit(solution)/shard_map/all_gather | solution.py:107
  25.9 115.0 %all-gather.9.cloned.1.call-start = ((), (), s32[]{:S(2)}) async-start(), calls=%async_computation.9 | async-start | bytes 2228224 | tf_op jit(solution)/shard_map/all_gather | solution.py:135
  26.5 3.4 %copy-start.1 = (bf16[4096,1024]{1,0:T(8,128)(2,1)S(1)}, bf16[4096,1024]{1,0:T(8,128)(2,1)}, u32[]{:S(2)}) copy-start(bf16[4096,1024]{1,0:T(8,128)(2,1)} %image_ref.1) | copy-start | bytes 25165828
  34.1 23.2 %collective-permute-start = (bf16[128,4096]{1,0:T(8,128)(2,1)S(1)}, bf16[128,4096]{1,0:T(8,128)(2,1)S(1)}, u32[]{:S(2)}, u32[]{:S(2)}) collective-permute-start(bf16[128,4096]{1,0:T(8,128)(2,1)S(1)} %project_kv.1), channel_id=1, source_target_pairs={{0,16},{16,0},{1,17},{17,1},{2,18},{18,2},{3,19},{19,3},{4,20},{20... | collective-permute-start | bytes 3145736 | tf_op jit(solution)/shard_map/ppermute | solution.py:140
  34.8 9.0 %copy-start.5 = (bf16[1024,64]{0,1:T(8,128)(2,1)S(1)}, bf16[1024,64]{0,1:T(8,128)(2,1)}, u32[]{:S(2)}) copy-start(bf16[1024,64]{0,1:T(8,128)(2,1)} %param.11) | copy-start | bytes 393220
  45.1 24.0 %all-to-all-start.1 = ((bf16[8,64,512]{2,1,0:T(8,128)(2,1)}), bf16[8,64,512]{2,1,0:T(8,128)(2,1)S(1)}, u32[]{:S(2)}, u32[]{:S(2)}) async-start(bf16[8,64,512]{2,1,0:T(8,128)(2,1)} %broadcast_in_dim.34), calls=%async_computation.1 | async-start | bytes 1048576 | tf_op jit(solution)/shard_map/all_to_all | solution.py:99
  52.6 96.0 %all-gather.15.cloned.1.call-start = ((), (), s32[]{:S(2)}) async-start(), calls=%async_computation.12 | async-start | bytes 1572864 | tf_op jit(solution)/shard_map/all_gather | solution.py:107
  99.6 41.3 %copy-start.3 = (bf16[3,1024,64]{1,2,0:T(8,128)(2,1)S(1)}, bf16[3,1024,64]{1,2,0:T(8,128)(2,1)}, u32[]{:S(2)}) copy-start(bf16[3,1024,64]{1,2,0:T(8,128)(2,1)} %param.14) | copy-start | bytes 1179652
  140.3 75.7 %all-gather.11.cloned.1.call-start = ((), (), s32[]{:S(2)}) async-start(), calls=%async_computation.10 | async-start | bytes 2228224 | tf_op jit(solution)/shard_map/all_gather | solution.py:136
  154.0 9.5 %all-to-all-start.4 = ((bf16[4,64,512]{2,1,0:T(8,128)(2,1)}), bf16[4,64,512]{2,1,0:T(8,128)(2,1)S(1)}, u32[]{:S(2)}, u32[]{:S(2)}) async-start(bf16[4,64,512]{2,1,0:T(8,128)(2,1)} %broadcast_in_dim.38), calls=%async_computation.4 | async-start | bytes 524288 | tf_op jit(solution)/shard_map/all_to_all | solution.py:99
  158.2 68.4 %all-gather.17.cloned.1.call-start = ((), (), s32[]{:S(2)}) async-start(), calls=%async_computation.13 | async-start | bytes 1572864 | tf_op jit(solution)/shard_map/all_gather | solution.py:107
  229.9 1.3 copy-start.2
  229.9 1.7 copy-start.6
  234.5 2.0 collective-permute-start.1
  237.5 18.1 %all-to-all-start.8 = ((bf16[8,32,1024]{2,1,0:T(8,128)(2,1)}), bf16[8,32,1024]{2,1,0:T(8,128)(2,1)S(1)}, u32[]{:S(2)}, u32[]{:S(2)}) async-start(bf16[8,32,1024]{2,1,0:T(8,128)(2,1)} %fusion.4), calls=%async_computation.8 | async-start | bytes 1048576 | tf_op jit(solution)/shard_map/all_to_all | solution.py:99
Sparse Core Ops, SparseCore 0:
  26.0 12.8 all-gather.12
  41.6 53.8 all-gather.8
  140.4 8.1 all-gather.14
  151.2 54.6 all-gather.10
  216.0 10.5 all-gather.16
